TPU v7x, 512 devices: a whole 4x4x16 slice. The times are simulated.
512 devices in a mesh: row: 8 (over x, core), col: 64 (over y, z).
Axes of the slice: x: 4, y: 4, z: 16, core: 2. Of those that a mesh axis runs over, the one named last changes fastest.
Arguments:
- diag_factors: bfloat16 [3, 512, 512], replicated, as said below
- panel_v: bfloat16 [64, 2, 512, 128], P('row', None, 'col'), may hold values from -2.515625 to 2.515625
- ranks: int32 [64, 2], P('row'), may hold values from 32 to 128, as said below
Outputs:
- panel_factors: bfloat16 [64, 1024, 256], P('row', 'col')
- update_cores: float32 [64, 64, 256, 256], P('row', 'col')
Inputs may be any that keep to these rules, and one draw needn't show every extreme that they name: `ranks`: every panel tile has rank at least 32; the tiles of array row 0 have rank 128. `diag_factors`: inverse0 and inverse1 are lower triangular with positive diagonals.
All inputs are finite; a program needn't handle non-finite values.
Results may differ from a plain program's by a relative error of at most 0.0046.
Values may be sent and summed in bfloat16 or wider, within the bound.
No kernel may reach another device: no remote copies, remote signals or barrier semaphores. Data moves between devices by JAX's collectives and lax.ppermute only.
A program may use at most 64 MiB of HBM per device.

v0:
```python
import jax
import jax.numpy as jnp
from jax import lax
from jax.sharding import PartitionSpec as P


def from_root(block, axis, source):
    block = jnp.where(lax.axis_index(axis) == source, block, jnp.zeros_like(block))
    return lax.psum(block, axis)


def assemble(w_block, lower, right):
    top = jnp.concatenate([w_block, jnp.zeros_like(w_block)], axis=-1)
    bottom = jnp.concatenate([lower, right], axis=-1)
    return jnp.concatenate([top, bottom], axis=-2)


def shards(diag_factors, panel_v, ranks):
    rows_dev = panel_v.shape[0]
    rank_max = panel_v.shape[3]
    nrow = lax.axis_size("row")
    ncol = lax.axis_size("col")
    prow = lax.axis_index("row")
    qcol = lax.axis_index("col")
    inverse0 = diag_factors[0]
    couple = diag_factors[1]
    inverse1 = diag_factors[2]
    columns = jnp.arange(rank_max, dtype=jnp.int32)
    keep = columns[None, None, :] < ranks[:, :, None]
    masked = jnp.where(keep[:, :, None, :], panel_v, jnp.zeros_like(panel_v))
    whole = lax.all_gather(masked, "col", axis=2, tiled=True)
    w_block = jnp.einsum(
        "nm,tmr->tnr", inverse0, whole[:, 0], preferred_element_type=jnp.float32
    ).astype(jnp.bfloat16)
    right = jnp.einsum(
        "nm,tmr->tnr", inverse1, whole[:, 1], preferred_element_type=jnp.float32
    ).astype(jnp.bfloat16)
    lower = jnp.einsum("nm,tmr->tnr", couple, w_block, preferred_element_type=jnp.float32).astype(
        jnp.bfloat16
    )
    factors = assemble(w_block, lower, right)
    piece = factors.shape[1] // ncol
    factor_share = lax.dynamic_slice_in_dim(factors, qcol * piece, piece, 1)
    owner = qcol % nrow
    local_row = qcol // nrow
    picked = lax.dynamic_index_in_dim(factors, local_row, 0, keepdims=False)
    column_factor = from_root(picked, "row", owner)
    cores = jnp.einsum("tkr,ks->trs", factors, column_factor, preferred_element_type=jnp.float32)
    codes = jnp.arange(rows_dev, dtype=jnp.int32) * nrow + prow
    active = codes > qcol
    cores = jnp.where(active[:, None, None], cores, jnp.zeros_like(cores))
    return (factor_share, cores[:, None])


def solution(mesh):
    placed = (P(), P("row", None, "col", None), P("row", None))
    return jax.shard_map(
        shards,
        mesh=mesh,
        in_specs=placed,
        out_specs=(P("row", "col", None), P("row", "col", None, None)),
        check_vma=False,
    )
```

profile of v0, /device:TPU:8, one launch (start us, length us, event | category | flops | bytes accessed | tf_op | source)
XLA Modules:
  0.0 252.6 jit_solution(16143106622238425557)
XLA Ops:
  7.2 0.0 all-gather.2.cloned.1.call-start
  7.2 0.8 iota_compare_fusion.1
  8.0 1.4 copy_select_fusion
  9.3 0.0 all-gather.2.cloned.1.call-update
  9.4 0.0 all-reduce.3.cloned.1.call-start
  9.4 146.3 %all-gather.2.cloned.1.call-done = bf16[8,2,512,128]{3,0,1,2:T(8,128)(2,1)} async-done(((bf16[8,2,8,128]{3,0,1,2:T(8,128)(2,1)}), bf16[8,2,512,128]{3,0,1,2:T(8,128)(2,1)}) %all-gather.2.cloned.1.call-update) | async-done | bytes 2097168 | tf_op jit(solution)/shard_map/all_gather | solution.py:31
  155.8 1.7 fusion.15
  157.4 0.7 copy.17
  158.1 0.7 copy.18
  158.8 1.8 fusion.2
  160.6 1.8 fusion.4
  162.4 1.8 fusion.3
  164.2 0.0 copy-start.1
  164.2 1.0 copy-done.1
  165.1 0.5 fusion.1
  165.7 0.0 copy-start
  165.7 1.9 copy-done
  167.6 0.8 select_bitcast_fusion.1
  168.4 0.0 all-reduce.3.cloned.1.call-update
  168.5 1.3 constant_dynamic-slice_fusion
  169.7 0.8 copy.13
  170.6 71.2 %all-reduce.3.cloned.1.call-done = bf16[1024,256]{0,1:T(8,128)(2,1)} async-done(((bf16[1024,256]{0,1:T(8,128)(2,1)}), bf16[1024,256]{0,1:T(8,128)(2,1)}) %all-reduce.3.cloned.1.call-update) | async-done | bytes 524304 | tf_op jit(solution)/shard_map/psum | solution.py:9
  241.8 4.0 %select_bitcast_fusion = f32[8,1,256,256]{3,2,1,0:T(8,128)} fusion(pred[8]{0:T(512)(128)(4,1)S(1)} %add_compare_fusion, bf16[1024,256]{0,1:T(8,128)(2,1)} %all-reduce.3.cloned.1.call-done, bf16[8,512,128]{1,2,0:T(8,128)(2,1)S(1)} %fusion.2, bf16[8,512,128]{1,2,0:T(8,128)(2,1)S(1)} %fusion.4, bf16[8,512,128]{1,2,0:T(8,128)(2,1)} %copy-done.1), kind=kOutput, calls=%fused_computation.3 | convolution fusion | flops 1091043328 | bytes 5767176 | tf_op jit(solution)/shard_map/tkr,ks->trs/dot_general | solution.py:48
  (1 shorter events, 0.0 us)
Async XLA Ops:
  7.2 148.6 %all-gather.2.cloned.1.call-start = ((), (), s32[]{:S(2)}) async-start(), calls=%async_computation | async-start | bytes 2129920 | tf_op jit(solution)/shard_map/all_gather | solution.py:31
  9.4 232.4 %all-reduce.3.cloned.1.call-start = ((), (), s32[]{:S(2)}) async-start(), calls=%async_computation.1 | async-start | bytes 1048576 | tf_op jit(solution)/shard_map/psum | solution.py:9
  164.2 1.0 copy-start.1
  165.7 1.9 copy-start
Sparse Core Ops, SparseCore 0:
  11.5 144.1 all-gather.1
  168.6 73.1 all-reduce.2
where the time goes:
time: 253 us
  waiting for transfers between devices  218 us (86%)
  between operations  14.1 us (6%)
  matrix products  9.31 us (4%)
  local copies, waits for them, and re-layouts  8.01 us (3%)
  other arithmetic  3.49 us (1%)
    all_gather x1, waiting for transfers between devices, shards(): whole = lax.all_gather(masked, 'col', axis=2, tiled=True)  146 us
    psum x1, waiting for transfers between devices, from_root(): return lax.psum(block, axis)  71.2 us
    unnamed x7, local copies, waits for them, and re-layouts  5.07 us
  transfers between devices with their start and end apart: 2, of which 2 were waited for; matrix products, arithmetic and copies ran while one was open for 1% of the time, Pallas kernels for 0%

commit v1 on v0

--- a/solution.py
+++ b/solution.py
@@ -2,6 +2,13 @@
 import jax.numpy as jnp
 from jax import lax
 from jax.sharding import PartitionSpec as P
+
+end_sizes_now = lambda buf, dimension_no: jnp.concatenate(
+    jax.lax.all_to_all(
+        jnp.stack(jax.lax.axis_size("col") * [buf], axis=0), "col", split_axis=0, concat_axis=0
+    ),
+    axis=dimension_no,
+)
 
 
 def from_root(block, axis, source):
@@ -28,7 +35,7 @@
     columns = jnp.arange(rank_max, dtype=jnp.int32)
     keep = columns[None, None, :] < ranks[:, :, None]
     masked = jnp.where(keep[:, :, None, :], panel_v, jnp.zeros_like(panel_v))
-    whole = lax.all_gather(masked, "col", axis=2, tiled=True)
+    whole = end_sizes_now(masked, 2)
     w_block = jnp.einsum(
         "nm,tmr->tnr", inverse0, whole[:, 0], preferred_element_type=jnp.float32
     ).astype(jnp.bfloat16)

time: 253 us -> 216 us (0.85)
  waiting for transfers between devices: 218 us -> 165 us
  starting transfers between devices: 0.08 us -> 18.8 us
  matrix products: 9.31 us -> 6.22 us
    all_gather x1 -> x0, waiting for transfers between devices: 146 us -> none  [shards(): whole = lax.all_gather(masked, 'col', axis=2, tiled=True)]
    all_to_all x0 -> x1, waiting for transfers between devices: none -> 97.4 us  [jax.lax.all_to_all(jnp.stack(jax.lax.axis_size('col') * [buf], axis=0), '...]
    all_to_all x0 -> x1, starting transfers between devices: none -> 18.7 us  [jax.lax.all_to_all(jnp.stack(jax.lax.axis_size('col') * [buf], axis=0), '...]
    psum x1, waiting for transfers between devices: 71.2 us -> 67.8 us  [from_root(): return lax.psum(block, axis)]
    unnamed x7 -> x8, local copies, waits for them, and re-layouts: 5.07 us -> 5.33 us
where the time goes in v1:
time: 216 us
  waiting for transfers between devices  165 us (76%)
  starting transfers between devices  18.8 us (9%)
  between operations  14.1 us (7%)
  local copies, waits for them, and re-layouts  8.95 us (4%)
  matrix products  6.22 us (3%)
  other arithmetic  2.21 us (1%)
    all_to_all x1, waiting for transfers between devices, jax.lax.all_to_all(jnp.stack(jax.lax.axis_size('col') * [buf], axis=0), '...  97.4 us
    psum x1, waiting for transfers between devices, from_root(): return lax.psum(block, axis)  67.8 us
    all_to_all x1, starting transfers between devices, jax.lax.all_to_all(jnp.stack(jax.lax.axis_size('col') * [buf], axis=0), '...  18.7 us
    unnamed x8, local copies, waits for them, and re-layouts  5.33 us
  transfers between devices with their start and end apart: 2, of which 2 were waited for; matrix products, arithmetic and copies ran while one was open for 1% of the time, Pallas kernels for 0%

profile of v1, /device:TPU:8, one launch (start us, length us, event | category | flops | bytes accessed | tf_op | source)
XLA Modules:
  0.0 215.5 jit_solution(7039342695954034531)
XLA Ops:
  7.2 0.8 copy.16
  7.9 0.1 iota_compare_fusion.1
  8.0 0.8 broadcast_select_fusion
  8.8 1.8 stack.2
  10.6 18.7 %all-to-all-start = ((bf16[64,8,2,8,128]{4,3,2,1,0:T(8,128)(2,1)}), bf16[64,8,2,8,128]{4,3,2,1,0:T(8,128)(2,1)S(1)}, u32[]{:S(2)}, u32[]{:S(2)}) async-start(bf16[64,8,2,8,128]{4,3,2,1,0:T(8,128)(2,1)} %stack.2), calls=%async_computation | async-start | bytes 4194304 | tf_op jit(solution)/shard_map/all_to_all | solution.py:7
  29.3 0.0 all-reduce.3.cloned.1.call-start
  29.4 97.4 %all-to-all-done = bf16[64,8,2,8,128]{4,3,2,1,0:T(8,128)(2,1)S(1)} async-done(((bf16[64,8,2,8,128]{4,3,2,1,0:T(8,128)(2,1)}), bf16[64,8,2,8,128]{4,3,2,1,0:T(8,128)(2,1)S(1)}, u32[]{:S(2)}, u32[]{:S(2)}) %all-to-all-start) | async-done | bytes 2097184 | tf_op jit(solution)/shard_map/all_to_all | solution.py:7
  126.8 0.0 copy-start.2
  126.8 0.5 copy.28
  127.4 0.9 copy-done.2
  128.3 0.8 fusion.2
  129.0 0.8 fusion.4
  129.8 0.7 fusion.3
  130.5 0.0 copy-start.1
  130.5 1.0 copy-done.1
  131.5 0.5 fusion.1
  132.0 0.0 copy-start
  132.0 1.9 copy-done
  134.0 0.8 select_bitcast_fusion.1
  134.8 0.0 all-reduce.3.cloned.1.call-update
  134.8 1.3 constant_dynamic-slice_fusion
  136.1 0.8 copy.21
  136.9 67.8 %all-reduce.3.cloned.1.call-done = bf16[1024,256]{0,1:T(8,128)(2,1)} async-done(((bf16[1024,256]{0,1:T(8,128)(2,1)}), bf16[1024,256]{0,1:T(8,128)(2,1)}) %all-reduce.3.cloned.1.call-update) | async-done | bytes 524304 | tf_op jit(solution)/shard_map/psum | solution.py:16
  204.7 4.0 %select_bitcast_fusion = f32[8,1,256,256]{3,2,1,0:T(8,128)} fusion(pred[8]{0:T(512)(128)(4,1)S(1)} %add_compare_fusion, bf16[1024,256]{0,1:T(8,128)(2,1)} %all-reduce.3.cloned.1.call-done, bf16[8,512,128]{1,2,0:T(8,128)(2,1)S(1)} %fusion.2, bf16[8,512,128]{1,2,0:T(8,128)(2,1)S(1)} %fusion.4, bf16[8,512,128]{1,2,0:T(8,128)(2,1)} %copy-done.1), kind=kOutput, calls=%fused_computation.4 | convolution fusion | flops 1091043328 | bytes 5767176 | tf_op jit(solution)/shard_map/tkr,ks->trs/dot_general | solution.py:55
  (1 shorter events, 0.0 us)
Async XLA Ops:
  10.6 116.2 %all-to-all-start = ((bf16[64,8,2,8,128]{4,3,2,1,0:T(8,128)(2,1)}), bf16[64,8,2,8,128]{4,3,2,1,0:T(8,128)(2,1)S(1)}, u32[]{:S(2)}, u32[]{:S(2)}) async-start(bf16[64,8,2,8,128]{4,3,2,1,0:T(8,128)(2,1)} %stack.2), calls=%async_computation | async-start | bytes 4194304 | tf_op jit(solution)/shard_map/all_to_all | solution.py:7
  29.3 175.4 %all-reduce.3.cloned.1.call-start = ((), (), s32[]{:S(2)}) async-start(), calls=%async_computation.1 | async-start | bytes 1048576 | tf_op jit(solution)/shard_map/psum | solution.py:16
  126.8 1.4 copy-start.2
  130.5 1.0 copy-start.1
  132.0 1.9 copy-start
Sparse Core Ops, SparseCore 0:
  134.9 69.7 all-reduce.2

commit v2 on v0

--- a/solution.py
+++ b/solution.py
@@ -3,10 +3,12 @@
 from jax import lax
 from jax.sharding import PartitionSpec as P
 
+remake_the_ladders = lambda original, shard_axis: lax.all_gather(original, shard_axis).sum(axis=0)
+
 
 def from_root(block, axis, source):
     block = jnp.where(lax.axis_index(axis) == source, block, jnp.zeros_like(block))
-    return lax.psum(block, axis)
+    return remake_the_ladders(block, axis)
 
 
 def assemble(w_block, lower, right):

time: 253 us -> 223 us (0.88)
  the two profiles are of different devices: /device:TPU:8 before, /device:TPU:1 now
where the time goes in v2:
time: 223 us; the launch traced here: 222 us
  waiting for transfers between devices  183 us (82%)
  between operations  14.1 us (6%)
  local copies, waits for them, and re-layouts  9.87 us (4%)
  matrix products  9.09 us (4%)
  other arithmetic  6.41 us (3%)
    all_gather x1, waiting for transfers between devices, shards(): whole = lax.all_gather(masked, 'col', axis=2, tiled=True)  140 us
    all_gather x1, waiting for transfers between devices, lax.all_gather(original, shard_axis).sum(axis=0)  43.1 us
    unnamed x9, local copies, waits for them, and re-layouts  5.9 us
  transfers between devices with their start and end apart: 2, of which 2 were waited for; matrix products, arithmetic and copies ran while one was open for 1% of the time, Pallas kernels for 0%

profile of v2, /device:TPU:1, one launch (start us, length us, event | category | flops | bytes accessed | tf_op | source)
XLA Modules:
  0.0 222.2 jit_solution(14660856804563983273)
XLA Ops:
  7.2 0.0 all-gather.3.cloned.1.call-start
  7.2 0.8 iota_compare_fusion.1
  8.0 1.4 copy_select_fusion
  9.3 0.0 all-gather.3.cloned.1.call-update
  9.4 0.0 all-gather.5.cloned.1.call-start
  9.4 139.5 %all-gather.3.cloned.1.call-done = bf16[8,2,512,128]{3,0,1,2:T(8,128)(2,1)} async-done(((bf16[8,2,8,128]{3,0,1,2:T(8,128)(2,1)}), bf16[8,2,512,128]{3,0,1,2:T(8,128)(2,1)}) %all-gather.3.cloned.1.call-update) | async-done | bytes 2097168 | tf_op jit(solution)/shard_map/all_gather | solution.py:33
  149.0 1.7 fusion.15
  150.7 0.7 copy.19
  151.4 1.5 copy.20
  152.8 1.8 fusion.2
  154.6 2.1 fusion.4
  156.7 1.8 fusion.3
  158.5 0.0 copy-start.1
  158.5 1.0 copy-done.1
  159.5 0.5 fusion.1
  160.0 0.0 copy-start
  160.0 2.0 copy-done
  162.0 1.0 copy.11
  163.1 0.0 all-gather.5.cloned.1.call-update
  163.1 1.3 constant_dynamic-slice_fusion
  164.4 0.8 copy.14
  165.2 0.0 copy-start.2
  165.2 43.1 %all-gather.5.cloned.1.call-done = bf16[8,1024,256]{2,1,0:T(8,128)(2,1)} async-done(((bf16[1,1024,256]{2,1,0:T(8,128)(2,1)}), bf16[8,1024,256]{2,1,0:T(8,128)(2,1)}) %all-gather.5.cloned.1.call-update) | async-done | bytes 4194320 | tf_op jit(solution)/shard_map/all_gather | solution.py:6
  208.3 3.7 %reduce_sum.12 = bf16[1024,256]{1,0:T(8,128)(2,1)} reduce(bf16[8,1024,256]{2,1,0:T(8,128)(2,1)} %all-gather.5.cloned.1.call-done, bf16[]{:T(256)} %constant.40.clone.1), dimensions={0}, to_apply=%region_0.1 | reduce | flops 1835008 | bytes 4718594 | tf_op jit(solution)/shard_map/reduce_sum | solution.py:6
  212.0 0.0 copy-done.2
  212.0 3.4 %select_bitcast_fusion = f32[8,1,256,256]{3,2,1,0:T(8,128)} fusion(pred[8]{0:T(512)(128)(4,1)S(1)} %add_compare_fusion, bf16[1024,256]{1,0:T(8,128)(2,1)} %reduce_sum.12, bf16[8,512,128]{1,2,0:T(8,128)(2,1)S(1)} %fusion.2, bf16[8,512,128]{1,2,0:T(8,128)(2,1)S(1)} %fusion.4, bf16[8,512,128]{1,2,0:T(8,128)(2,1)S(1)} %copy-done.2), kind=kOutput, calls=%fused_computation.3 | convolution fusion | flops 1091043328 | bytes 5767176 | tf_op jit(solution)/shard_map/tkr,ks->trs/dot_general | solution.py:50
  (2 shorter events, 0.1 us)
Async XLA Ops:
  7.2 141.8 %all-gather.3.cloned.1.call-start = ((), (), s32[]{:S(2)}) async-start(), calls=%async_computation | async-start | bytes 2129920 | tf_op jit(solution)/shard_map/all_gather | solution.py:33
  9.4 198.9 %all-gather.5.cloned.1.call-start = ((), (), s32[]{:S(2)}) async-start(), calls=%async_computation.1 | async-start | bytes 4718592 | tf_op jit(solution)/shard_map/all_gather | solution.py:6
  158.5 1.0 copy-start.1
  160.0 2.0 copy-start
  165.2 46.8 %copy-start.2 = (bf16[8,512,128]{1,2,0:T(8,128)(2,1)S(1)}, bf16[8,512,128]{1,2,0:T(8,128)(2,1)}, u32[]{:S(2)}) copy-start(bf16[8,512,128]{1,2,0:T(8,128)(2,1)} %copy-done.1) | copy-start | bytes 3145732
Sparse Core Ops, SparseCore 0:
  11.5 137.4 all-gather.2
  163.2 45.0 all-gather.4
